TPU v7x, 32 devices: a whole 2x2x4 slice. The times are simulated.
32 devices in a mesh: grp: 2 (over x), tok: 16 (over z, y, core).
Axes of the slice: x: 2, y: 2, z: 4, core: 2. Of those that a mesh axis runs over, the one named last changes fastest.
Arguments:
- frames: bfloat16 [256, 48, 4096], P(('grp', 'tok')), parts along dimension 0, may hold values from -6 to 6
- clip_lengths: int32 [8], P('grp'), parts along dimension 0, may hold values from 1 to 56, as said below
- sequence_slot_map: int32 [2048], P(('grp', 'tok')), parts along dimension 0, may hold values from 0 to 1023, as said below
- stem_weight: bfloat16 [128, 48], replicated, may hold values from -0.875 to 0.875
- time_weight: bfloat16 [3, 128, 128], replicated, may hold values from -0.3125 to 0.3125
- norm_gain: float32 [128], replicated, may hold values from 0.1 to 1.9
- mid_weight: bfloat16 [512, 2048], replicated, may hold values from -0.125 to 0.125
- latent_weight: bfloat16 [16, 4096], replicated, may hold values from -0.09375 to 0.09375
- patch_embed_weight: bfloat16 [64, 2048], replicated, may hold values from -0.75 to 0.75
Outputs:
- dit_rows: bfloat16 [2048, 2048], P(('grp', 'tok')), parts along dimension 0
There are 2 independent parts, one for each index of `grp`. A program takes and returns all parts, laid end to end along the dimension named above; an argument that names none is the same for every part. Nothing has to cross between parts.
Inputs may be any that keep to these rules, and one draw needn't show every extreme that they name: `clip_lengths`: clips fill the 16 slabs in order: the counts ceil(length / 8) sum to 16. `sequence_slot_map`: A permutation of the 1024 sequence slots. The rows of one slab send at most 8 rows to the slots of any one slab (exactly 8 to some), and how many slab s sends to slab (s + k) mod 16 depends on k only.
All inputs are finite; a program needn't handle non-finite values.
Results may differ from a plain program's by a relative error of at most 0.0071.
Values may be sent and summed in bfloat16 or wider, within the bound.
A program may use at most 128 MiB of HBM per device.

v0:
```python
import jax
import jax.numpy as jnp
from jax import lax
from jax.sharding import PartitionSpec as P

LS = 16


def shifted(block, axis, distance):
    devices = range(lax.axis_size(axis))
    route = [(i - distance, i) for i in devices if i - distance in devices]
    return lax.ppermute(block, axis, route)


def project(weight, data):
    return jnp.einsum("oc,fcp->fop", weight, data, preferred_element_type=jnp.float32)


def deliver(select, payload):
    packed = jnp.dot(select.astype(jnp.bfloat16), payload, preferred_element_type=jnp.float32)
    return packed.astype(jnp.bfloat16)


def per_device(
    frames,
    clip_lengths,
    sequence_slot_map,
    stem_weight,
    time_weight,
    norm_gain,
    mid_weight,
    latent_weight,
    patch_embed_weight,
):
    slab = lax.axis_index("tok")
    ndev = lax.axis_size("tok")
    count_frames = frames.shape[0]
    counts = (clip_lengths + 7) // 8
    ends = jnp.cumsum(counts)
    which = jnp.sum((ends <= slab).astype(jnp.int32))
    hot = jnp.arange(clip_lengths.shape[0], dtype=jnp.int32) == which
    start = jnp.sum(jnp.where(hot, ends - counts, 0))
    length = jnp.sum(jnp.where(hot, clip_lengths, 0))
    live = jnp.clip(length - count_frames * (slab - start), 0, count_frames)
    valid = (jnp.arange(count_frames, dtype=jnp.int32) < live).astype(jnp.float32)
    keep = jnp.where(slab == start, jnp.float32(0.0), jnp.float32(1.0))
    first_section = (project(stem_weight, frames) * valid[:, None, None]).astype(jnp.bfloat16)
    arrived = shifted(first_section[count_frames - 2 :], "tok", 1)
    prior = (arrived.astype(jnp.float32) * keep).astype(jnp.bfloat16)
    joined = jnp.concatenate([prior, first_section], axis=0)
    mixed = project(time_weight[0], joined[2 : count_frames + 2])
    mixed = mixed + project(time_weight[1], joined[1 : count_frames + 1])
    mixed = mixed + project(time_weight[2], joined[0:count_frames])
    meansq = jnp.mean(mixed * mixed, axis=1, keepdims=True)
    normed = mixed * lax.rsqrt(meansq + 1e-06) * norm_gain[None, :, None]
    activated = (normed * jax.nn.sigmoid(normed)).astype(jnp.bfloat16)
    channels = activated.shape[1]
    side = LS
    regrouped = activated.reshape(count_frames, channels * 16, side * side)
    deep = project(mid_weight, regrouped)
    deep = (deep * jax.nn.sigmoid(deep)).astype(jnp.bfloat16)
    latent_channels = latent_weight.shape[0]
    taps = latent_weight.reshape(latent_channels, count_frames, deep.shape[1])
    latent = jnp.einsum("ofc,fcp->op", taps, deep, preferred_element_type=jnp.float32).astype(
        jnp.bfloat16
    )
    half = side // 2
    rows = (
        latent.reshape(latent_channels, half, 2, half, 2)
        .transpose(1, 3, 0, 2, 4)
        .reshape(half * half, latent_channels * 4)
    )
    rows_count = rows.shape[0]
    capacity = max(2, 2 * rows_count // ndev)
    target = sequence_slot_map // rows_count
    place = sequence_slot_map % rows_count
    onehot = (target[:, None] == jnp.arange(ndev, dtype=jnp.int32)[None, :]).astype(jnp.int32)
    rank = jnp.sum(jnp.cumsum(onehot, axis=0) * onehot, axis=1) - 1
    send_index = target * capacity + rank
    select = send_index[None, :] == jnp.arange(ndev * capacity, dtype=jnp.int32)[:, None]
    slot_tags = jnp.sum(jnp.where(select, place[None, :] + 1, 0), axis=1).reshape(ndev, capacity)
    ordering_indices = jnp.arange(rows_count, dtype=jnp.int32)[:, None] + 1
    width = rows.shape[1]
    outgoing = deliver(select, rows).reshape(ndev, capacity, width)
    incoming, tags = (
        lax.all_to_all(outgoing, "tok", split_axis=0, concat_axis=0, tiled=True),
        lax.all_to_all(slot_tags, "tok", split_axis=0, concat_axis=0, tiled=True),
    )
    arrange = tags.reshape(1, -1) == ordering_indices
    placed = deliver(arrange, incoming.reshape(ndev * capacity, width))
    return jnp.dot(placed, patch_embed_weight, preferred_element_type=jnp.float32).astype(
        jnp.bfloat16
    )


def solution(mesh):
    placed = (
        P(("grp", "tok"), None, None),
        P("grp"),
        P(("grp", "tok")),
        P(),
        P(),
        P(),
        P(),
        P(),
        P(),
    )
    return jax.shard_map(
        per_device, mesh=mesh, in_specs=placed, out_specs=P(("grp", "tok"), None), check_vma=False
    )
```

profile of v0, /device:TPU:0, one launch (start us, length us, event | category | flops | bytes accessed | tf_op | source)
XLA Modules:
  0.0 121.0 jit_solution(15784494415079990977)
XLA Ops:
  0.0 0.0 copy-start
  0.0 0.0 copy-start.7
  0.0 0.0 copy-start.4
  0.0 0.8 fusion.55
  0.8 0.2 reduce-window.9
  1.0 0.6 fusion.46
  1.6 2.0 %fusion.43 = (s32[]{:T(128)}, s32[]{:T(128)}) fusion(s32[4]{0:T(128)} %param.10, s32[]{:T(128)} %fusion.46, s32[4,1]{0,1:T(1,128)S(1)} %reduce-window.9), kind=kLoop, calls=%fused_computation.61 | loop fusion | flops 86 | bytes 44 | tf_op jit(solution)/shard_map/reduce_sum | solution.py:43
  5.0 0.0 copy-done
  5.0 4.1 %fusion.5 = bf16[8,128,4096]{1,2,0:T(8,128)(2,1)S(1)} fusion(f32[8]{0:T(128)S(1)} %compare_convert_fusion, bf16[8,48,4096]{2,1,0:T(8,128)(2,1)S(1)} %copy-done, bf16[128,48]{0,1:T(8,128)(2,1)} %param.12), kind=kOutput, calls=%fused_computation.11 | convolution fusion | flops 411041792 | bytes 11546656 | tf_op jit(solution)/shard_map/oc,fcp->fop/dot_general | solution.py:16
  9.1 0.0 copy-start.2
  9.1 3.2 %copy-done.2 = bf16[8,128,4096]{1,2,0:T(8,128)(2,1)} copy-done((bf16[8,128,4096]{1,2,0:T(8,128)(2,1)}, bf16[8,128,4096]{1,2,0:T(8,128)(2,1)S(1)}, u32[]{:S(2)}) %copy-start.2) | copy-done | bytes 8388632
  12.3 0.1 slice.24
  12.4 3.7 %collective-permute-start = (bf16[2,128,4096]{1,2,0:T(8,128)(2,1)S(1)}, bf16[2,128,4096]{1,2,0:T(8,128)(2,1)}, u32[]{:S(2)}, u32[]{:S(2)}) collective-permute-start(bf16[2,128,4096]{1,2,0:T(8,128)(2,1)S(1)} %slice.24), channel_id=1, source_target_pairs={{0,1},{1,2},{2,3},{3,4},{4,5},{5,6},{6,7},{7,8},{8,9},{9,10},{10,1... | collective-permute-start | bytes 6291464 | tf_op jit(solution)/shard_map/ppermute | solution.py:12
  16.2 0.0 copy-done.7
  16.2 0.1 fusion.34
  16.3 0.1 reduce_window_sum.18
  16.3 0.2 select_reduce_fusion.1
  16.5 0.1 select_reduce_fusion
  16.6 0.7 all_to_all.9
  17.3 5.9 %all-to-all-start = ((s32[16,1,8]{2,1,0:T(1,128)}), s32[16,1,8]{2,1,0:T(1,128)S(1)}, u32[]{:S(2)}, u32[]{:S(2)}) async-start(s32[16,1,8]{2,1,0:T(1,128)} %bitcast), calls=%async_computation | async-start | bytes 16384 | tf_op jit(solution)/shard_map/all_to_all | solution.py:87
  23.9 0.0 copy-done.4
  23.9 0.0 copy-start.3
  23.9 11.6 %fusion.29 = f32[8,4096,128]{1,2,0:T(8,128)} fusion(bf16[8,128,4096]{1,2,0:T(8,128)(2,1)} %copy-done.2, bf16[3,128,128]{2,1,0:T(8,128)(2,1)S(1)} %copy-done.4), kind=kOutput, calls=%fused_computation.33 | convolution fusion | flops 1073741824 | bytes 25198592 | tf_op jit(solution)/shard_map/oc,fcp->fop/dot_general | solution.py:16
  35.5 0.0 collective-permute-done
  35.5 2.0 %multiply_convert_fusion.1 = bf16[2,128,4096]{1,2,0:T(8,128)(2,1)S(1)} fusion(bf16[2,128,4096]{1,2,0:T(8,128)(2,1)} %collective-permute-done, f32[]{:T(128)S(6)} %select_n.38), kind=kLoop, calls=%fused_computation.17 | loop fusion | flops 3145728 | bytes 4194308 | tf_op jit(solution)/shard_map/convert_element_type | solution.py:49
  37.5 0.0 copy-done.3
  37.5 7.0 %fusion.4 = f32[8,4096,128]{1,2,0:T(8,128)} fusion(bf16[8,128,4096]{1,2,0:T(8,128)(2,1)S(1)} %copy-done.3, bf16[2,128,4096]{1,2,0:T(8,128)(2,1)S(1)} %multiply_convert_fusion.1, bf16[3,128,128]{2,1,0:T(8,128)(2,1)S(1)} %copy-done.4), kind=kOutput, calls=%fused_computation.10 | convolution fusion | flops 1094713344 | bytes 27295744 | tf_op jit(solution)/shard_map/oc,fcp->fop/dot_general | solution.py:16
  44.5 20.3 %multiply_reduce_fusion = (f32[8,4096]{1,0:T(8,128)S(1)}, f32[8,4096,128]{1,2,0:T(8,128)}) fusion(bf16[3,128,128]{2,1,0:T(8,128)(2,1)S(1)} %copy-done.4, bf16[8,128,4096]{1,2,0:T(8,128)(2,1)} %copy-done.2, bf16[2,128,4096]{1,2,0:T(8,128)(2,1)S(1)} %multiply_convert_fusion.1, f32[8,4096,128]{1,2,0:T(8,128)} %fusion.29, f32[8,4096,128]{1,2,0:T(8,128)} %fusion.4), kind=kOutput, calls=%fused_computation.5 | convolution fusion | flops 1111457792 | bytes 60981248 | tf_op jit(solution)/shard_map/oc,fcp->fop/dot_general | solution.py:16
  64.8 0.0 copy-done.5
  64.8 11.6 %fusion.3 = bf16[8,128,4096]{2,1,0:T(8,128)(2,1)} fusion(f32[8,4096,128]{1,2,0:T(8,128)} %get-tuple-element.8, f32[128]{0:T(128)S(1)} %copy-done.5, f32[8,4096]{1,0:T(8,128)S(1)} %add_rsqrt_fusion), kind=kLoop, calls=%fused_computation.8 | loop fusion | flops 29360128 | bytes 25297408 | tf_op jit(solution)/shard_map/convert_element_type | solution.py:56
  76.4 13.5 %reshape.76 = bf16[8,2048,256]{2,1,0:T(8,128)(2,1)} reshape(bf16[8,128,4096]{2,1,0:T(8,128)(2,1)} %fusion.3) | data formatting | bytes 16777216 | tf_op jit(solution)/shard_map/reshape | solution.py:59
  89.9 0.0 copy-done.6
  89.9 8.9 %fusion.20 = bf16[16,256]{1,0:T(8,128)(2,1)S(1)} fusion(bf16[8,2048,256]{2,1,0:T(8,128)(2,1)} %reshape.76, bf16[512,2048]{1,0:T(8,128)(2,1)} %param.15, bf16[2,8,8,512]{3,2,1,0:T(8,128)(2,1)S(1)} %bitcast.103), kind=kOutput, calls=%fused_computation.26 | convolution fusion | flops 4333768704 | bytes 10625024 | tf_op jit(solution)/shard_map/ofc,fcp->op/dot_general | solution.py:64
  98.8 0.1 copy.42
  98.9 0.3 copy.43
  99.2 0.1 reshape.79
  99.3 0.2 convolution_convert_fusion.2
  99.5 0.1 copy.44
  99.7 0.7 reshape.97
  100.4 0.0 all-to-all-done
  100.4 11.9 %all-to-all-start.1 = ((bf16[16,2,256]{2,1,0:T(2,128)(2,1)}), bf16[16,2,256]{2,1,0:T(2,128)(2,1)S(1)}, u32[]{:S(2)}, u32[]{:S(2)}) async-start(bf16[16,2,256]{2,1,0:T(2,128)(2,1)} %reshape.97), calls=%async_computation.1 | async-start | bytes 32768 | tf_op jit(solution)/shard_map/all_to_all | solution.py:86
  112.3 0.6 broadcast.108
  112.9 0.7 reduce.4
  113.6 0.1 eq.58
  113.7 5.1 %all-to-all-done.1 = bf16[16,2,256]{2,1,0:T(2,128)(2,1)S(1)} async-done(((bf16[16,2,256]{2,1,0:T(2,128)(2,1)}), bf16[16,2,256]{2,1,0:T(2,128)(2,1)S(1)}, u32[]{:S(2)}, u32[]{:S(2)}) %all-to-all-start.1) | async-done | bytes 16416 | tf_op jit(solution)/shard_map/all_to_all | solution.py:86
  118.8 0.1 reshape.98
  118.9 2.1 %convolution_convert_fusion = bf16[64,2048]{1,0:T(8,128)(2,1)} fusion(bf16[64,2048]{1,0:T(8,128)(2,1)} %param.17, bf16[16,8,64]{2,1,0:T(8,128)(2,1)S(1)} %reshape.98, s32[128]{0:T(128)S(1)} %eq.58, s32[64]{0:T(128)S(1)} %iota_add_fusion), kind=kOutput, calls=%fused_computation.19 | convolution fusion | flops 17969152 | bytes 541440 | tf_op jit(solution)/shard_map/dot_general | solution.py:91
  121.0 0.0 copy-done.1
  (8 shorter events, 0.1 us)
Async XLA Ops:
  0.0 5.0 %copy-start = (bf16[8,48,4096]{2,1,0:T(8,128)(2,1)S(1)}, bf16[8,48,4096]{2,1,0:T(8,128)(2,1)}, u32[]{:S(2)}) copy-start(bf16[8,48,4096]{2,1,0:T(8,128)(2,1)} %param.9) | copy-start | bytes 9437188
  0.0 16.2 %copy-start.7 = (s32[64]{0:T(128)S(1)}, s32[64]{0:T(128)}, u32[]{:S(2)}) copy-start(s32[64]{0:T(128)} %param.11) | copy-start | bytes 772
  0.0 23.9 %copy-start.4 = (bf16[3,128,128]{2,1,0:T(8,128)(2,1)S(1)}, bf16[3,128,128]{2,1,0:T(8,128)(2,1)}, u32[]{:S(2)}) copy-start(bf16[3,128,128]{2,1,0:T(8,128)(2,1)} %param.13) | copy-start | bytes 294916
  9.1 3.2 %copy-start.2 = (bf16[8,128,4096]{1,2,0:T(8,128)(2,1)}, bf16[8,128,4096]{1,2,0:T(8,128)(2,1)S(1)}, u32[]{:S(2)}) copy-start(bf16[8,128,4096]{1,2,0:T(8,128)(2,1)S(1)} %fusion.5) | copy-start | bytes 25165828
  12.4 23.0 %collective-permute-start = (bf16[2,128,4096]{1,2,0:T(8,128)(2,1)S(1)}, bf16[2,128,4096]{1,2,0:T(8,128)(2,1)}, u32[]{:S(2)}, u32[]{:S(2)}) collective-permute-start(bf16[2,128,4096]{1,2,0:T(8,128)(2,1)S(1)} %slice.24), channel_id=1, source_target_pairs={{0,1},{1,2},{2,3},{3,4},{4,5},{5,6},{6,7},{7,8},{8,9},{9,10},{10,1... | collective-permute-start | bytes 6291464 | tf_op jit(solution)/shard_map/ppermute | solution.py:12
  17.3 83.1 %all-to-all-start = ((s32[16,1,8]{2,1,0:T(1,128)}), s32[16,1,8]{2,1,0:T(1,128)S(1)}, u32[]{:S(2)}, u32[]{:S(2)}) async-start(s32[16,1,8]{2,1,0:T(1,128)} %bitcast), calls=%async_computation | async-start | bytes 16384 | tf_op jit(solution)/shard_map/all_to_all | solution.py:87
  23.9 13.6 %copy-start.3 = (bf16[8,128,4096]{1,2,0:T(8,128)(2,1)S(1)}, bf16[8,128,4096]{1,2,0:T(8,128)(2,1)}, u32[]{:S(2)}) copy-start(bf16[8,128,4096]{1,2,0:T(8,128)(2,1)} %copy-done.2) | copy-start | bytes 25165828
  44.5 20.3 %copy-start.5 = (f32[128]{0:T(128)S(1)}, f32[128]{0:T(128)}, u32[]{:S(2)}) copy-start(f32[128]{0:T(128)} %param.14) | copy-start | bytes 1540
  76.4 13.5 %copy-start.6 = (bf16[16,4096]{1,0:T(8,128)(2,1)S(1)}, bf16[16,4096]{1,0:T(8,128)(2,1)}, u32[]{:S(2)}) copy-start(bf16[16,4096]{1,0:T(8,128)(2,1)} %param.16) | copy-start | bytes 393220
  89.9 31.1 %copy-start.1 = (bf16[8,48,4096]{2,1,0:T(8,128)(2,1)S(1)}, bf16[8,48,4096]{2,1,0:T(8,128)(2,1)}, u32[]{:S(2)}) copy-start(bf16[8,48,4096]{2,1,0:T(8,128)(2,1)} %param.9) | copy-start | bytes 9437188
  100.4 18.4 %all-to-all-start.1 = ((bf16[16,2,256]{2,1,0:T(2,128)(2,1)}), bf16[16,2,256]{2,1,0:T(2,128)(2,1)S(1)}, u32[]{:S(2)}, u32[]{:S(2)}) async-start(bf16[16,2,256]{2,1,0:T(2,128)(2,1)} %reshape.97), calls=%async_computation.1 | async-start | bytes 32768 | tf_op jit(solution)/shard_map/all_to_all | solution.py:86
where the time goes:
time: 122 us; the launch traced here: 121 us
  matrix products  54.1 us (44%)
  starting transfers between devices  21.5 us (18%)
  local copies, waits for them, and re-layouts  19.7 us (16%)
  other arithmetic  18.4 us (15%)
  waiting for transfers between devices  5.09 us (4%)
  between operations  2.09 us (2%)
    dot_general x4, matrix products, project(): jnp.einsum('oc,fcp->fop', weight, data, preferred_element_type=jnp.float32)  43 us
    reshape x1, local copies, waits for them, and re-layouts, per_device(): regrouped = activated.reshape(count_frames, channels * 16, side * side)  13.5 us
    all_to_all x1, starting transfers between devices, per_device(): lax.all_to_all(outgoing, 'tok', split_axis=0, concat_axis=0, tiled=True)  11.9 us
    convert_element_type x1, other arithmetic, per_device(): activated = (normed * jax.nn.sigmoid(normed)).astype(jnp.bfloat16)  11.6 us
    dot_general x1, matrix products, per_device(): jnp.einsum('ofc,fcp->op', taps, deep, preferred_element_type=jnp.float32)  8.92 us
    all_to_all x1, starting transfers between devices, per_device(): lax.all_to_all(slot_tags, 'tok', split_axis=0, concat_axis=0, tiled=True)  5.89 us
    all_to_all x1, waiting for transfers between devices, per_device(): lax.all_to_all(outgoing, 'tok', split_axis=0, concat_axis=0, tiled=True)  5.09 us
    unnamed x18, local copies, waits for them, and re-layouts  4.03 us
  transfers between devices with their start and end apart: 3, of which 1 were waited for; matrix products, arithmetic and copies ran while one was open for 65% of the time, Pallas kernels for 0%

commit v1 on v0

v1 whole, which is shorter than its diff:
```python
import functools

import jax
import jax.numpy as jnp
from jax import lax
from jax.experimental import pallas as pl
from jax.experimental.pallas import tpu as pltpu
from jax.sharding import PartitionSpec as P

F32 = jnp.float32
BF16 = jnp.bfloat16
I32 = jnp.int32
SPAN = 3


def iota(shape, dim):
    return lax.broadcasted_iota(I32, shape, dim)


def dot(a, b, contract=((1,), (0,))):
    return lax.dot_general(a, b, (contract, ((), ())), preferred_element_type=F32)


def shift_of(size):
    assert size & (size - 1) == 0
    return size.bit_length() - 1


def kernel(
    n, side, clip_ref, slot_hbm, gain_hbm, frames_hbm, stem_hbm, time_hbm, mid_hbm, lat_hbm, pe_hbm,
    out_ref,
    slot, gain, frames, stem, time, mid, lat, pe,
    toeplitz, masked, wide_gain, mid_perm, pe_perm, select, s_ref, outbuf, inbuf,
    load_sem, carry_sems, send_sem, recv_sem,
):
    me = lax.axis_index("tok")
    nframes, cin, _ = frames_hbm.shape
    c1 = stem_hbm.shape[0]
    cells = side * side
    blocks = frames_hbm.shape[2] // cells
    c2 = mid_hbm.shape[0]
    latc = lat_hbm.shape[0]
    rows = slot_hbm.shape[1]
    cap = outbuf.shape[1]
    width = outbuf.shape[2]
    slots = n * cap
    features = pe_hbm.shape[0]
    quads = features // latc

    loads = [
        pltpu.make_async_copy(stem_hbm, stem, load_sem.at[0]),
        pltpu.make_async_copy(time_hbm, time, load_sem.at[1]),
        pltpu.make_async_copy(gain_hbm, gain, load_sem.at[2]),
        pltpu.make_async_copy(frames_hbm.at[0:5], frames.at[2:7], load_sem.at[3]),
        pltpu.make_async_copy(mid_hbm, mid, load_sem.at[4]),
        pltpu.make_async_copy(slot_hbm, slot, load_sem.at[5]),
        pltpu.make_async_copy(frames_hbm.at[5:nframes], frames.at[7 : nframes + 2], load_sem.at[6]),
        pltpu.make_async_copy(pe_hbm, pe, load_sem.at[7]),
    ] + [
        pltpu.make_async_copy(lat_hbm.at[:, f * c2 : (f + 1) * c2], lat.at[f], load_sem.at[8 + f])
        for f in range(nframes)
    ]
    for load in loads:
        load.start()

    barrier = pltpu.get_barrier_semaphore()

    def greet(k, _):
        pl.semaphore_signal(
            barrier, inc=1, device_id={"tok": lax.rem(me + k, n)}, device_id_type=pl.DeviceIdType.MESH
        )
        return 0

    lax.fori_loop(1, n, greet, 0)
    pl.semaphore_wait(barrier, n - 1)

    carry = pltpu.make_async_remote_copy(
        src_ref=frames_hbm.at[nframes - 2 : nframes],
        dst_ref=frames.at[0:2],
        send_sem=carry_sems.at[0],
        recv_sem=carry_sems.at[1],
        device_id={"tok": lax.rem(me + 1, n)},
        device_id_type=pl.DeviceIdType.MESH,
    )

    @pl.when(me < n - 1)
    def _():
        carry.start()

    @pl.when(me == 0)
    def _():
        frames[0:2] = jnp.zeros_like(frames[0:2])

    start = jnp.int32(0)
    end = jnp.int32(0)
    live = jnp.int32(0)
    keep = jnp.float32(1.0)
    for c in range(clip_ref.shape[0]):
        length = clip_ref[c]
        start = end
        end = end + lax.div(length + (nframes - 1), jnp.int32(nframes))
        inside = jnp.logical_and(start <= me, me < end)
        live = jnp.where(inside, jnp.clip(length - nframes * (me - start), 0, nframes), live)
        keep = jnp.where(jnp.logical_and(inside, start == me), jnp.float32(0.0), keep)

    kspan = (SPAN + 2) * cin
    loads[0].wait()
    loads[1].wait()
    placed_stem = [
        dot(stem[...], (iota((cin, kspan), 1) == iota((cin, kspan), 0) + b * cin).astype(BF16)).astype(BF16)
        for b in range(SPAN + 2)
    ]
    for j in range(SPAN):
        row = dot(time[2], placed_stem[j]) + dot(time[1], placed_stem[j + 1]) + dot(time[0], placed_stem[j + 2])
        toeplitz[j * c1 : (j + 1) * c1, :] = row.astype(BF16)

    loads[2].wait()
    diagonal = iota((c1, c1), 0) == iota((c1, c1), 1)
    column = jnp.sum(jnp.where(diagonal, jnp.broadcast_to(gain[...], (c1, c1)), 0.0), axis=1, keepdims=True)
    wide_gain[...] = jnp.broadcast_to(0.5 * column, wide_gain.shape)

    loads[4].wait()
    chunk = 16 * blocks
    k_in, k_out = iota((chunk, chunk), 0), iota((chunk, chunk), 1)
    bits = shift_of(blocks)
    swap = ((k_in >> bits) == (k_out & 15)) & ((k_in & (blocks - 1)) == (k_out >> 4))
    swap = swap.astype(BF16)
    for q in range(c1 // 16):
        at = slice(q * chunk, (q + 1) * chunk)
        mid_perm[:, at] = dot(mid[:, at], swap).astype(BF16)

    loads[5].wait()
    row_bits = shift_of(rows)
    where_to = slot[...]
    target = where_to >> row_bits
    place = where_to & (rows - 1)
    onehot = iota((n, rows), 0) == target
    before = (iota((rows, rows), 0) < iota((rows, rows), 1)).astype(BF16)
    earlier = dot(onehot.astype(BF16), before)
    rank = jnp.sum(jnp.where(onehot, earlier, 0.0), axis=0, keepdims=True).astype(I32)
    select[...] = (iota((slots, rows), 0) == target * cap + rank).astype(BF16)

    loads[7].wait()
    f_out, f_in = iota((width, features), 0), iota((width, features), 1)
    latc_bits, quad_bits = shift_of(latc), shift_of(quads)
    reorder = (f_out >> latc_bits == (f_in & (quads - 1))) & ((f_out & (latc - 1)) == f_in >> quad_bits)
    pe_perm[...] = dot(reorder.astype(BF16), pe[...]).astype(BF16)

    for f in range(nframes):
        loads[8 + f].wait()

    def group(first, count, latent):
        column_id = iota((1, kspan), 1)
        on = jnp.where(column_id < cin * (live - first + 2), jnp.float32(1.0), jnp.float32(0.0))
        on = jnp.where(column_id < cin * (2 - first), keep, on)
        masked[...] = (toeplitz[...].astype(F32) * on).astype(BF16)
        m_rows, k_rows = count * c1, (count + 2) * cin

        def conv(ab, _):
            at = pl.ds(pl.multiple_of(ab * cells, cells), cells)
            data = frames[first : first + count + 2, :, at].reshape(k_rows, cells)
            h = dot(masked[0:m_rows, 0:k_rows], data)
            for j in range(count):
                hj = h[j * c1 : (j + 1) * c1]
                scale = lax.rsqrt(jnp.sum(hj * hj, axis=0, keepdims=True) * (1.0 / c1) + 1e-6)
                x = hj * scale * wide_gain[...]
                u = x + x * jnp.tanh(x)
                s_ref[j, :, ab] = u.astype(BF16).reshape(c1 // 16, 16, cells)
            return 0

        lax.fori_loop(0, blocks, conv, 0, unroll=2)

        def deep(j, acc):
            g = 0.5 * dot(mid_perm[...], s_ref[j].reshape(c1 * blocks, cells))
            m = (g + g * jnp.tanh(g)).astype(BF16)
            return acc + dot(lat[first + j], m)

        return lax.fori_loop(0, count, deep, latent)

    latent = jnp.zeros((latc, cells), F32)
    loads[3].wait()
    latent = group(2, 3, latent)
    loads[6].wait()
    latent = group(5, 3, latent)

    @pl.when(me > 0)
    def _():
        carry.wait_recv()

    latent = group(0, 2, latent)

    half = side // 2
    half_bits = shift_of(half)
    cell, row_id = iota((cells, rows), 0), iota((cells, rows), 1)
    latent = latent.astype(BF16)
    parts = []
    for q in range(quads):
        a, b = q // 2, q % 2
        pick = cell == (2 * (row_id >> half_bits) + a) * side + 2 * (row_id & (half - 1)) + b
        parts.append(dot(latent, pick.astype(BF16)))
    tag = jnp.where(iota((width - features, rows), 0) == 0, (place + 1).astype(F32), 0.0)
    rows_t = jnp.concatenate(parts + [tag], axis=0).astype(BF16)
    payload = dot(select[...], rows_t, ((1,), (1,)))
    outbuf[...] = payload.reshape(n, cap, width)

    def exchange(k):
        to = lax.rem(me + k, n)
        return pltpu.make_async_remote_copy(
            src_ref=outbuf.at[to],
            dst_ref=inbuf.at[me],
            send_sem=send_sem.at[k],
            recv_sem=recv_sem.at[k],
            device_id={"tok": to},
            device_id_type=pl.DeviceIdType.MESH,
        )

    def send(k, _):
        exchange(k).start()
        return 0

    def finish(k, _):
        exchange(k).wait()
        return 0

    lax.fori_loop(1, n, send, 0)
    inbuf[me] = outbuf[me]
    lax.fori_loop(1, n, finish, 0)

    arrived = inbuf[...].reshape(slots, width)
    arrange = (arrived[:, features : features + 1] == (iota((slots, rows), 1) + 1).astype(F32)).astype(BF16)
    placed = dot(arrange, arrived.astype(BF16), ((0,), (0,))).astype(BF16)
    out_ref[...] = dot(placed, pe_perm[...]).astype(BF16)

    @pl.when(me < n - 1)
    def _():
        carry.wait_send()


def per_device(n, frames, clip_lengths, slot_map, stem, time, gain, mid, lat, pe):
    nframes, cin, pos = frames.shape
    c1, c2, latc = stem.shape[0], mid.shape[0], lat.shape[0]
    blocks = mid.shape[1] // c1
    cells = pos // blocks
    side = int(round(cells**0.5))
    rows = slot_map.shape[0]
    features, wide = pe.shape
    width = 2 * features
    cap = -(-max(2, 2 * rows // n) // 8) * 8
    vmem = pltpu.VMEM
    anywhere = pl.BlockSpec(memory_space=pl.ANY)
    kspan = (SPAN + 2) * cin
    return pl.pallas_call(
        functools.partial(kernel, n, side),
        out_shape=jax.ShapeDtypeStruct((rows, wide), BF16),
        in_specs=[pl.BlockSpec(memory_space=pltpu.SMEM)] + [anywhere] * 8,
        out_specs=pl.BlockSpec(memory_space=vmem),
        scratch_shapes=[
            vmem((1, rows), I32),
            vmem((1, c1), F32),
            vmem((nframes + 2, cin, pos), BF16),
            vmem(stem.shape, BF16),
            vmem(time.shape, BF16),
            vmem(mid.shape, BF16),
            vmem((nframes, latc, c2), BF16),
            vmem(pe.shape, BF16),
            vmem((SPAN * c1, kspan), BF16),
            vmem((SPAN * c1, kspan), BF16),
            vmem((c1, cells), F32),
            vmem(mid.shape, BF16),
            vmem((width, wide), BF16),
            vmem((n * cap, rows), BF16),
            vmem((SPAN, c1 // 16, blocks, 16, cells), BF16),
            vmem((n, cap, width), F32),
            vmem((n, cap, width), F32),
            pltpu.SemaphoreType.DMA((8 + nframes,)),
            pltpu.SemaphoreType.DMA((2,)),
            pltpu.SemaphoreType.DMA((n,)),
            pltpu.SemaphoreType.DMA((n,)),
        ],
        compiler_params=pltpu.CompilerParams(
            collective_id=0, has_side_effects=True, vmem_limit_bytes=56 * 2**20
        ),
        cost_estimate=pl.CostEstimate(
            flops=2 * nframes * (pos * c1 * 3 * cin + cells * c2 * c1 * blocks),
            bytes_accessed=2 * (nframes * cin * pos + mid.size + pe.size + rows * wide),
            transcendentals=nframes * pos * c1,
        ),
    )(clip_lengths, slot_map.reshape(1, rows), gain.reshape(1, c1), frames, stem, time, mid, lat, pe)


def solution(mesh):
    sharded = P(("grp", "tok"), None, None)
    return jax.shard_map(
        functools.partial(per_device, mesh.shape["tok"]),
        mesh=mesh,
        in_specs=(sharded, P("grp"), P(("grp", "tok")), P(), P(), P(), P(), P(), P()),
        out_specs=P(("grp", "tok"), None),
        check_vma=False,
    )
```

time: 122 us -> 33.7 us (0.28)
  matrix products: 54.1 us -> 0 us
  Pallas kernels: 0 us -> 30.3 us
  starting transfers between devices: 21.5 us -> 0 us
  other arithmetic: 18.4 us -> 0 us
  local copies, waits for them, and re-layouts: 19.7 us -> 3.09 us
  waiting for transfers between devices: 5.09 us -> 0 us
  between operations: 2.09 us -> 0.01 us
    dot_general x7 -> x0, matrix products: 54.1 us -> none  [the longest x4 43 us: project(): jnp.einsum('oc,fcp->fop', weight, data, preferred_element_type=jnp.float32)]
    pallas_call x0 -> x1, Pallas kernels: none -> 30.3 us  [per_device(): pl.pallas_call(functools.partial(kernel, n, side), out_shape=jax.ShapeDty...]
    all_to_all x2 -> x0, starting transfers between devices: 17.8 us -> none  [the longest x1 11.9 us: per_device(): lax.all_to_all(outgoing, 'tok', split_axis=0, concat_axis=0, tiled=True)]
    convert_element_type x4 -> x0, other arithmetic: 13.6 us -> none  [the longest x1 11.6 us: per_device(): activated = (normed * jax.nn.sigmoid(normed)).astype(jnp.bfloat16)]
    reshape x2 -> x0, local copies, waits for them, and re-layouts: 13.6 us -> none  [the longest x1 13.5 us: per_device(): regrouped = activated.reshape(count_frames, channels * 16, side * side)]
    all_to_all x2 -> x0, waiting for transfers between devices: 5.09 us -> none  [the longest x1 5.09 us: per_device(): lax.all_to_all(outgoing, 'tok', split_axis=0, concat_axis=0, tiled=True)]
    ppermute x1 -> x0, starting transfers between devices: 3.73 us -> none  [shifted(): return lax.ppermute(block, axis, route)]
    reduce_sum x4 -> x0, other arithmetic: 2.94 us -> none  [the longest x1 2.02 us: per_device(): length = jnp.sum(jnp.where(hot, clip_lengths, 0))]
  transfers between devices with their start and end apart: 3 -> 0, of which waited for: 1 -> 0; matrix products, arithmetic and copies ran while one was open for 65% -> 0% of each run, Pallas kernels for 0% -> 0%
where the time goes in v1:
time: 33.7 us; the launch traced here: 33.4 us
  Pallas kernels  30.3 us (90%)
  local copies, waits for them, and re-layouts  3.09 us (9%)
    pallas_call x1, Pallas kernels, per_device(): pl.pallas_call(functools.partial(kernel, n, side), out_shape=jax.ShapeDty...  30.3 us
    unnamed x2, local copies, waits for them, and re-layouts  3.09 us

profile of v1, /device:TPU:0, one launch (start us, length us, event | category | flops | bytes accessed | tf_op | source)
XLA Modules:
  0.0 33.4 jit_solution(2264746657407054645)
XLA Ops:
  0.0 1.4 %copy.10.stem_hbm = bf16[128,48]{1,0:T(8,128)(2,1)} copy(bf16[128,48]{0,1:T(8,128)(2,1)} %param.12) | data formatting | bytes 24576 | tf_op args[3]
  1.4 30.3 %shard_map.91 = bf16[64,2048]{1,0:T(8,128)(2,1)} custom-call(s32[4]{0:T(128)} %clip_ref.1, s32[1,64]{1,0:T(1,128)} %bitcast.2, f32[1,128]{1,0:T(1,128)} %bitcast.3, bf16[8,48,4096]{2,1,0:T(8,128)(2,1)} %frames_hbm.1, bf16[128,48]{1,0:T(8,128)(2,1)} %copy.10.stem_hbm, bf16[3,128,128]{2,1,0:T(8,128)(2,1)} %time_hbm.1, bf16[512,2048]{1,0:T(8,128)(2,1)} %mid_hbm.1, ...), custom_call_target="tpu_custom_call" | custom-call | flops 5502926848 | bytes 5767168 | tf_op jit(solution)/shard_map/pallas_call | solution.py:252
  31.8 1.7 %copy.12 = bf16[64,2048]{1,0:T(8,128)(2,1)} copy(bf16[64,2048]{1,0:T(8,128)(2,1)} %shard_map.91) | data formatting | bytes 524288

commit v2 on v1

v2 whole, which is shorter than its diff:
```python
import functools

import jax
import jax.numpy as jnp
from jax import lax
from jax.experimental import pallas as pl
from jax.experimental.pallas import tpu as pltpu
from jax.sharding import PartitionSpec as P

F32 = jnp.float32
BF16 = jnp.bfloat16
I32 = jnp.int32
SPAN = 2


def iota(shape, dim):
    return lax.broadcasted_iota(I32, shape, dim)


def dot(a, b, contract=((1,), (0,))):
    return lax.dot_general(a, b, (contract, ((), ())), preferred_element_type=F32)


def shift_of(size):
    assert size & (size - 1) == 0
    return size.bit_length() - 1


def kernel(
    n, side, clip_ref, slot_hbm, gain_hbm, frames_hbm, stem_hbm, time_hbm, mid_hbm, lat_hbm,
    out_ref,
    slot, gain, frames, stem, time, mid, lat,
    toeplitz, masked, wide_gain, swap, mid_perm, lat_rep, pick, select, s_ref, m_ref, outbuf, inbuf,
    load_sem, carry_send, carry_recv, send_sem, recv_sem,
):
    me = lax.axis_index("tok")
    nframes, cin, pos = frames_hbm.shape
    c1 = stem_hbm.shape[1]
    cells = side * side
    blocks = pos // cells
    c2 = mid_hbm.shape[0]
    latc = lat_hbm.shape[0]
    rows = slot_hbm.shape[1]
    cap = outbuf.shape[1]
    width = outbuf.shape[2]
    slots = n * cap
    quads = 4
    features = quads * latc
    tall = c2 // 2
    pieces = carry_send.shape[0]
    per_step = blocks // pieces
    groups = nframes // SPAN

    loads = [
        pltpu.make_async_copy(stem_hbm, stem, load_sem.at[0]),
        pltpu.make_async_copy(time_hbm, time, load_sem.at[1]),
        pltpu.make_async_copy(gain_hbm, gain, load_sem.at[2]),
        pltpu.make_async_copy(slot_hbm, slot, load_sem.at[3]),
        pltpu.make_async_copy(frames_hbm.at[0:4], frames.at[2:6], load_sem.at[4]),
        pltpu.make_async_copy(mid_hbm, mid, load_sem.at[5]),
        pltpu.make_async_copy(lat_hbm, lat, load_sem.at[6]),
        pltpu.make_async_copy(frames_hbm.at[4:nframes], frames.at[6 : nframes + 2], load_sem.at[7]),
    ]
    for load in loads:
        load.start()

    barrier = pltpu.get_barrier_semaphore()

    def greet(k, _):
        pl.semaphore_signal(
            barrier, inc=1, device_id={"tok": lax.rem(me + k, n)}, device_id_type=pl.DeviceIdType.MESH
        )
        return 0

    lax.fori_loop(1, n, greet, 0)

    @pl.when(me == 0)
    def _():
        frames[0:2] = jnp.zeros_like(frames[0:2])

    bits = shift_of(blocks)
    k_in, k_out = iota(swap.shape, 0), iota(swap.shape, 1)
    moved = ((k_in >> bits) == (k_out & 15)) & ((k_in & (blocks - 1)) == (k_out >> 4))
    swap[...] = jnp.where(moved, jnp.float32(0.5), jnp.float32(0.0)).astype(BF16)
    half = side // 2
    half_bits = shift_of(half)
    cell, row_id = iota((cells, rows), 0), iota((cells, rows), 1)
    for q in range(quads):
        a, b = q // 2, q % 2
        pick[q] = (cell == (2 * (row_id >> half_bits) + a) * side + 2 * (row_id & (half - 1)) + b).astype(BF16)

    pl.semaphore_wait(barrier, n - 1)

    wide_piece = pos // pieces

    def carry(p):
        at = pl.ds(pl.multiple_of(p * wide_piece, wide_piece), wide_piece)
        return pltpu.make_async_remote_copy(
            src_ref=frames_hbm.at[nframes - 2 : nframes, :, at],
            dst_ref=frames.at[0:2, :, at],
            send_sem=carry_send.at[p],
            recv_sem=carry_recv.at[p],
            device_id={"tok": lax.rem(me + 1, n)},
            device_id_type=pl.DeviceIdType.MESH,
        )

    @pl.when(me < n - 1)
    def _():
        for p in range(pieces):
            carry(p).start()

    start = jnp.int32(0)
    end = jnp.int32(0)
    live = jnp.int32(0)
    keep = jnp.float32(1.0)
    for c in range(clip_ref.shape[0]):
        length = clip_ref[c]
        start = end
        end = end + lax.div(length + (nframes - 1), jnp.int32(nframes))
        inside = jnp.logical_and(start <= me, me < end)
        live = jnp.where(inside, jnp.clip(length - nframes * (me - start), 0, nframes), live)
        keep = jnp.where(jnp.logical_and(inside, start == me), jnp.float32(0.0), keep)

    kspan = (SPAN + 2) * cin
    loads[0].wait()
    loads[1].wait()
    placed_stem = [
        dot(stem[...], (iota((cin, kspan), 1) == iota((cin, kspan), 0) + b * cin).astype(BF16), ((0,), (0,))).astype(BF16)
        for b in range(SPAN + 2)
    ]
    for j in range(SPAN):
        row = dot(time[2], placed_stem[j]) + dot(time[1], placed_stem[j + 1]) + dot(time[0], placed_stem[j + 2])
        toeplitz[j * c1 : (j + 1) * c1, :] = row
    column_id = iota((1, kspan), 1)
    for g in range(groups):
        first = (SPAN * (g + 1)) % nframes
        on = jnp.where(column_id < cin * (live - first + 2), jnp.float32(1.0), jnp.float32(0.0))
        on = jnp.where(column_id < cin * (2 - first), keep, on)
        masked[g] = (toeplitz[...] * on).astype(BF16)

    loads[2].wait()
    diagonal = iota((c1, c1), 0) == iota((c1, c1), 1)
    column = jnp.sum(jnp.where(diagonal, jnp.broadcast_to(gain[...], (c1, c1)), 0.0), axis=1, keepdims=True)
    wide_gain[...] = jnp.broadcast_to(0.5 * column, wide_gain.shape)

    loads[3].wait()
    row_bits = shift_of(rows)
    where_to = slot[...]
    target = where_to >> row_bits
    place = where_to & (rows - 1)
    onehot = iota((n, rows), 0) == target
    before = (iota((rows, rows), 0) < iota((rows, rows), 1)).astype(BF16)
    earlier = dot(onehot.astype(BF16), before)
    rank = jnp.sum(jnp.where(onehot, earlier, 0.0), axis=0, keepdims=True).astype(I32)
    select[...] = (iota((slots, rows), 0) == target * cap + rank).astype(BF16)

    m_ref[...] = jnp.zeros_like(m_ref)

    def conv(g, t):
        first = lax.rem(SPAN * (g + 1), nframes)
        weight = masked[g]
        for i in range(per_step):
            ab = t * per_step + i
            at = pl.ds(pl.multiple_of(ab * cells, cells), cells)
            data = frames[pl.ds(first, SPAN + 2), :, at].reshape(kspan, cells)
            h = dot(weight, data)
            for j in range(SPAN):
                hj = h[j * c1 : (j + 1) * c1]
                scale = lax.rsqrt(jnp.sum(hj * hj, axis=0, keepdims=True) * (1.0 / c1) + 1e-6)
                x = hj * scale * wide_gain[...]
                u = x + x * jnp.tanh(x)
                s_ref[first + j, :, ab] = u.astype(BF16).reshape(c1 // 16, 16, cells)

    def frame_of(unit):
        return lax.rem(SPAN + (unit >> 1), nframes)

    def gather_latent(unit, acc):
        at = frame_of(unit) * c2 + (unit & 1) * tall
        return acc + dot(lat_rep[:, pl.ds(pl.multiple_of(at, tall), tall)], m_ref[unit & 1])

    def deep(unit, acc):
        g = dot(mid_perm[unit & 1], s_ref[frame_of(unit)].reshape(c1 * blocks, cells))
        m_ref[unit & 1] = (g + g * jnp.tanh(g)).astype(BF16)
        return acc

    chunk = swap.shape[0]
    per_chunk = (c1 // 16) // pieces

    def opening(t, _):
        conv(0, t)
        for i in range(per_chunk):
            at = pl.ds(pl.multiple_of((t * per_chunk + i) * chunk, chunk), chunk)
            for top in range(2):
                mid_perm[top, :, at] = dot(mid[top * tall : (top + 1) * tall, at], swap[...]).astype(BF16)
        return 0

    loads[4].wait()
    loads[5].wait()
    lax.fori_loop(0, pieces, opening, 0)

    loads[6].wait()
    repeat = (iota((features, latc), 0) >> shift_of(quads) == iota((features, latc), 1)).astype(BF16)
    lat_rep[...] = dot(repeat, lat[...]).astype(BF16)
    loads[7].wait()

    step_bits = shift_of(pieces)

    def both(t, acc):
        acc = gather_latent(jnp.maximum(t - 1, 0), acc)
        conv(1 + (t >> step_bits), t & (pieces - 1))
        return deep(t, acc)

    middle = (groups - 2) * pieces
    acc = lax.fori_loop(0, middle, both, jnp.zeros((features, cells), F32))

    def with_carry(t, acc):
        @pl.when(me > 0)
        def _():
            carry(t).wait_recv()

        acc = gather_latent(middle + t - 1, acc)
        conv(groups - 1, t)
        return deep(middle + t, acc)

    acc = lax.fori_loop(0, pieces, with_carry, acc)

    def closing(t, acc):
        acc = gather_latent(middle + pieces + t - 1, acc)
        return deep(middle + pieces + t, acc)

    acc = lax.fori_loop(0, 2 * SPAN, closing, acc)
    latent = gather_latent(jnp.int32(2 * nframes - 1), acc).astype(BF16)

    quad = iota((features, rows), 0) & (quads - 1)
    picked = jnp.zeros((features, rows), F32)
    for q in range(quads):
        picked = jnp.where(quad == q, dot(latent, pick[q]), picked)
    tag = jnp.where(iota((width - features, rows), 0) == 0, (place + 1).astype(F32), 0.0)
    rows_t = jnp.concatenate([picked, tag], axis=0).astype(BF16)
    payload = dot(select[...], rows_t, ((1,), (1,)))
    outbuf[...] = payload.reshape(n, cap, width)

    def exchange(k):
        to = lax.rem(me + k, n)
        return pltpu.make_async_remote_copy(
            src_ref=outbuf.at[to],
            dst_ref=inbuf.at[me],
            send_sem=send_sem.at[k],
            recv_sem=recv_sem.at[k],
            device_id={"tok": to},
            device_id_type=pl.DeviceIdType.MESH,
        )

    def send(k, _):
        exchange(k).start()
        return 0

    def finish(k, _):
        exchange(k).wait()
        return 0

    lax.fori_loop(1, n, send, 0)
    inbuf[me] = outbuf[me]
    lax.fori_loop(1, n, finish, 0)

    arrived = inbuf[...].reshape(slots, width)
    arrange = (arrived[:, features : features + 1] == (iota((slots, rows), 1) + 1).astype(F32)).astype(BF16)
    placed = dot(arrange, arrived.astype(BF16), ((0,), (0,)))
    out_ref[...] = placed[:, 0:features].astype(BF16)

    @pl.when(me < n - 1)
    def _():
        for p in range(pieces):
            carry(p).wait_send()


def per_device(n, frames, clip_lengths, slot_map, stem, time, gain, mid, lat, pe):
    nframes, cin, pos = frames.shape
    c1, c2, latc = stem.shape[0], mid.shape[0], lat.shape[0]
    blocks = mid.shape[1] // c1
    cells = pos // blocks
    side = int(round(cells**0.5))
    rows = slot_map.shape[0]
    features = pe.shape[0]
    width = 2 * features
    pieces = 4
    cap = -(-max(2, 2 * rows // n) // 8) * 8
    vmem = pltpu.VMEM
    anywhere = pl.BlockSpec(memory_space=pl.ANY)
    kspan = (SPAN + 2) * cin
    placed = pl.pallas_call(
        functools.partial(kernel, n, side),
        out_shape=jax.ShapeDtypeStruct((rows, features), BF16),
        in_specs=[pl.BlockSpec(memory_space=pltpu.SMEM)] + [anywhere] * 7,
        out_specs=pl.BlockSpec(memory_space=vmem),
        scratch_shapes=[
            vmem((1, rows), I32),
            vmem((1, c1), F32),
            vmem((nframes + 2, cin, pos), BF16),
            vmem((cin, c1), BF16),
            vmem(time.shape, BF16),
            vmem(mid.shape, BF16),
            vmem(lat.shape, BF16),
            vmem((SPAN * c1, kspan), F32),
            vmem((nframes // SPAN, SPAN * c1, kspan), BF16),
            vmem((c1, cells), F32),
            vmem((16 * blocks, 16 * blocks), BF16),
            vmem((2, c2 // 2, mid.shape[1]), BF16),
            vmem((features, lat.shape[1]), BF16),
            vmem((4, cells, rows), BF16),
            vmem((n * cap, rows), BF16),
            vmem((nframes, c1 // 16, blocks, 16, cells), BF16),
            vmem((2, c2 // 2, cells), BF16),
            vmem((n, cap, width), F32),
            vmem((n, cap, width), F32),
            pltpu.SemaphoreType.DMA((8,)),
            pltpu.SemaphoreType.DMA((pieces,)),
            pltpu.SemaphoreType.DMA((pieces,)),
            pltpu.SemaphoreType.DMA((n,)),
            pltpu.SemaphoreType.DMA((n,)),
        ],
        compiler_params=pltpu.CompilerParams(
            collective_id=0, has_side_effects=True, vmem_limit_bytes=56 * 2**20
        ),
        cost_estimate=pl.CostEstimate(
            flops=2 * nframes * (pos * c1 * 3 * cin + cells * c2 * c1 * blocks),
            bytes_accessed=2 * (nframes * cin * pos + mid.size + rows * features),
            transcendentals=nframes * pos * c1,
        ),
    )(clip_lengths, slot_map.reshape(1, rows), gain.reshape(1, c1), frames, stem.T, time, mid, lat)
    return jnp.dot(placed, pe, preferred_element_type=F32).astype(BF16)


def solution(mesh):
    sharded = P(("grp", "tok"), None, None)
    return jax.shard_map(
        functools.partial(per_device, mesh.shape["tok"]),
        mesh=mesh,
        in_specs=(sharded, P("grp"), P(("grp", "tok")), P(), P(), P(), P(), P(), P()),
        out_specs=P(("grp", "tok"), None),
        check_vma=False,
    )
```

time: 33.7 us -> 31.5 us (0.935)
  local copies, waits for them, and re-layouts: 3.09 us -> 0.01 us
  matrix products: 0 us -> 1.63 us
  Pallas kernels: 30.3 us -> 29.6 us
    unnamed x2, local copies, waits for them, and re-layouts: 3.09 us -> 0.01 us
    dot_general x0 -> x1, matrix products: none -> 1.63 us  [per_device(): return jnp.dot(placed, pe, preferred_element_type=F32).astype(BF16)]
    pallas_call x1, Pallas kernels: 30.3 us -> 29.6 us  [per_device(): pl.pallas_call(functools.partial(kernel, n, side), out_shape=jax.ShapeDty...]
where the time goes in v2:
time: 31.5 us; the launch traced here: 31.2 us
  Pallas kernels  29.6 us (94%)
  matrix products  1.63 us (5%)
    pallas_call x1, Pallas kernels, per_device(): pl.pallas_call(functools.partial(kernel, n, side), out_shape=jax.ShapeDty...  29.6 us
    dot_general x1, matrix products, per_device(): return jnp.dot(placed, pe, preferred_element_type=F32).astype(BF16)  1.63 us

profile of v2, /device:TPU:0, one launch (start us, length us, event | category | flops | bytes accessed | tf_op | source)
XLA Modules:
  0.0 31.2 jit_solution(1912248314461480769)
XLA Ops:
  0.0 0.0 copy-start
  0.0 29.6 %shard_map.91 = bf16[64,64]{1,0:T(8,128)(2,1)} custom-call(s32[4]{0:T(128)} %clip_ref.1, s32[1,64]{1,0:T(1,128)} %bitcast.6, f32[1,128]{1,0:T(1,128)} %bitcast.7, bf16[8,48,4096]{2,1,0:T(8,128)(2,1)} %frames_hbm.1, bf16[48,128]{1,0:T(8,128)(2,1)} %bitcast.5, bf16[3,128,128]{2,1,0:T(8,128)(2,1)} %time_hbm.1, bf16[512,2048]{1,0:T(8,128)(2,1)} %mid_hbm.1, ...), custom_call_target="tpu_custom_call" | custom-call | flops 5502926848 | bytes 5251072 | tf_op jit(solution)/shard_map/pallas_call | solution.py:291
  29.6 0.0 copy-done
  29.6 1.6 %convolution_convert_fusion = bf16[64,2048]{1,0:T(8,128)(2,1)} fusion(bf16[64,64]{1,0:T(8,128)(2,1)} %shard_map.91, bf16[64,2048]{1,0:T(8,128)(2,1)S(1)} %copy-done), kind=kOutput, calls=%fused_computation | convolution fusion | flops 16908288 | bytes 532480 | tf_op jit(solution)/shard_map/dot_general | solution.py:331
Async XLA Ops:
  0.0 29.6 %copy-start = (bf16[64,2048]{1,0:T(8,128)(2,1)S(1)}, bf16[64,2048]{1,0:T(8,128)(2,1)}, u32[]{:S(2)}) copy-start(bf16[64,2048]{1,0:T(8,128)(2,1)} %param.17) | copy-start | bytes 786436

commit v3 on v2

--- a/solution.py
+++ b/solution.py
@@ -165,11 +165,13 @@
             data = frames[pl.ds(first, SPAN + 2), :, at].reshape(kspan, cells)
             h = dot(weight, data)
             for j in range(SPAN):
-                hj = h[j * c1 : (j + 1) * c1]
-                scale = lax.rsqrt(jnp.sum(hj * hj, axis=0, keepdims=True) * (1.0 / c1) + 1e-6)
-                x = hj * scale * wide_gain[...]
-                u = x + x * jnp.tanh(x)
-                s_ref[first + j, :, ab] = u.astype(BF16).reshape(c1 // 16, 16, cells)
+                for lane in range(0, cells, 128):
+                    hj = h[j * c1 : (j + 1) * c1, lane : lane + 128]
+                    scale = lax.rsqrt(jnp.sum(hj * hj, axis=0, keepdims=True) * (1.0 / c1) + 1e-6)
+                    for q in range(c1 // 16):
+                        x = hj[q * 16 : (q + 1) * 16] * scale * wide_gain[q * 16 : (q + 1) * 16, :]
+                        u = x + x * jnp.tanh(x)
+                        s_ref[first + j, q, ab, :, lane : lane + 128] = u.astype(BF16)
 
     def frame_of(unit):
         return lax.rem(SPAN + (unit >> 1), nframes)
@@ -180,7 +182,9 @@
 
     def deep(unit, acc):
         g = dot(mid_perm[unit & 1], s_ref[frame_of(unit)].reshape(c1 * blocks, cells))
-        m_ref[unit & 1] = (g + g * jnp.tanh(g)).astype(BF16)
+        for q in range(0, tall, 32):
+            part = g[q : q + 32]
+            m_ref[unit & 1, q : q + 32, :] = (part + part * jnp.tanh(part)).astype(BF16)
         return acc
 
     chunk = swap.shape[0]
@@ -303,7 +307,7 @@
             vmem(lat.shape, BF16),
             vmem((SPAN * c1, kspan), F32),
             vmem((nframes // SPAN, SPAN * c1, kspan), BF16),
-            vmem((c1, cells), F32),
+            vmem((c1, 128), F32),
             vmem((16 * blocks, 16 * blocks), BF16),
             vmem((2, c2 // 2, mid.shape[1]), BF16),
             vmem((features, lat.shape[1]), BF16),

time: 31.5 us -> 31.7 us (level)
  no operation moved by 1% of the time
where the time goes in v3:
time: 31.7 us; the launch traced here: 31.4 us
  Pallas kernels  29.8 us (94%)
  matrix products  1.63 us (5%)
    pallas_call x1, Pallas kernels, per_device(): pl.pallas_call(functools.partial(kernel, n, side), out_shape=jax.ShapeDty...  29.8 us
    dot_general x1, matrix products, per_device(): return jnp.dot(placed, pe, preferred_element_type=F32).astype(BF16)  1.63 us

profile of v3, /device:TPU:0, one launch (start us, length us, event | category | flops | bytes accessed | tf_op | source)
XLA Modules:
  0.0 31.4 jit_solution(15939204124608168880)
XLA Ops:
  0.0 0.0 copy-start
  0.0 29.8 %shard_map.91 = bf16[64,64]{1,0:T(8,128)(2,1)} custom-call(s32[4]{0:T(128)} %clip_ref.1, s32[1,64]{1,0:T(1,128)} %bitcast.6, f32[1,128]{1,0:T(1,128)} %bitcast.7, bf16[8,48,4096]{2,1,0:T(8,128)(2,1)} %frames_hbm.1, bf16[48,128]{1,0:T(8,128)(2,1)} %bitcast.5, bf16[3,128,128]{2,1,0:T(8,128)(2,1)} %time_hbm.1, bf16[512,2048]{1,0:T(8,128)(2,1)} %mid_hbm.1, ...), custom_call_target="tpu_custom_call" | custom-call | flops 5502926848 | bytes 5251072 | tf_op jit(solution)/shard_map/pallas_call | solution.py:295
  29.8 0.0 copy-done
  29.8 1.6 %convolution_convert_fusion = bf16[64,2048]{1,0:T(8,128)(2,1)} fusion(bf16[64,64]{1,0:T(8,128)(2,1)} %shard_map.91, bf16[64,2048]{1,0:T(8,128)(2,1)S(1)} %copy-done), kind=kOutput, calls=%fused_computation | convolution fusion | flops 16908288 | bytes 532480 | tf_op jit(solution)/shard_map/dot_general | solution.py:335
Async XLA Ops:
  0.0 29.8 %copy-start = (bf16[64,2048]{1,0:T(8,128)(2,1)S(1)}, bf16[64,2048]{1,0:T(8,128)(2,1)}, u32[]{:S(2)}) copy-start(bf16[64,2048]{1,0:T(8,128)(2,1)} %param.17) | copy-start | bytes 786436

commit v4 on v3

--- a/solution.py
+++ b/solution.py
@@ -19,6 +19,10 @@
 
 def dot(a, b, contract=((1,), (0,))):
     return lax.dot_general(a, b, (contract, ((), ())), preferred_element_type=F32)
+
+
+def wrap(index, size):
+    return jnp.where(index >= size, index - size, index)
 
 
 def shift_of(size):
@@ -46,9 +50,9 @@
     slots = n * cap
     quads = 4
     features = quads * latc
-    tall = c2 // 2
     pieces = carry_send.shape[0]
-    per_step = blocks // pieces
+    steps = 2
+    per_step = blocks // steps
     groups = nframes // SPAN
 
     loads = [
@@ -68,7 +72,7 @@
 
     def greet(k, _):
         pl.semaphore_signal(
-            barrier, inc=1, device_id={"tok": lax.rem(me + k, n)}, device_id_type=pl.DeviceIdType.MESH
+            barrier, inc=1, device_id={"tok": wrap(me + k, n)}, device_id_type=pl.DeviceIdType.MESH
         )
         return 0
 
@@ -100,7 +104,7 @@
             dst_ref=frames.at[0:2, :, at],
             send_sem=carry_send.at[p],
             recv_sem=carry_recv.at[p],
-            device_id={"tok": lax.rem(me + 1, n)},
+            device_id={"tok": wrap(me + 1, n)},
             device_id_type=pl.DeviceIdType.MESH,
         )
 
@@ -116,7 +120,7 @@
     for c in range(clip_ref.shape[0]):
         length = clip_ref[c]
         start = end
-        end = end + lax.div(length + (nframes - 1), jnp.int32(nframes))
+        end = end + ((length + (nframes - 1)) >> shift_of(nframes))
         inside = jnp.logical_and(start <= me, me < end)
         live = jnp.where(inside, jnp.clip(length - nframes * (me - start), 0, nframes), live)
         keep = jnp.where(jnp.logical_and(inside, start == me), jnp.float32(0.0), keep)
@@ -157,7 +161,7 @@
     m_ref[...] = jnp.zeros_like(m_ref)
 
     def conv(g, t):
-        first = lax.rem(SPAN * (g + 1), nframes)
+        first = (SPAN * (g + 1)) & (nframes - 1)
         weight = masked[g]
         for i in range(per_step):
             ab = t * per_step + i
@@ -174,66 +178,66 @@
                         s_ref[first + j, q, ab, :, lane : lane + 128] = u.astype(BF16)
 
     def frame_of(unit):
-        return lax.rem(SPAN + (unit >> 1), nframes)
+        return (SPAN + unit) & (nframes - 1)
 
     def gather_latent(unit, acc):
-        at = frame_of(unit) * c2 + (unit & 1) * tall
-        return acc + dot(lat_rep[:, pl.ds(pl.multiple_of(at, tall), tall)], m_ref[unit & 1])
+        at = frame_of(unit) * c2
+        return acc + dot(lat_rep[:, pl.ds(pl.multiple_of(at, c2), c2)], m_ref[unit & 1])
 
     def deep(unit, acc):
-        g = dot(mid_perm[unit & 1], s_ref[frame_of(unit)].reshape(c1 * blocks, cells))
-        for q in range(0, tall, 32):
+        g = dot(mid_perm[...], s_ref[frame_of(unit)].reshape(c1 * blocks, cells))
+        for q in range(0, c2, 32):
             part = g[q : q + 32]
             m_ref[unit & 1, q : q + 32, :] = (part + part * jnp.tanh(part)).astype(BF16)
         return acc
 
     chunk = swap.shape[0]
-    per_chunk = (c1 // 16) // pieces
+    per_chunk = (c1 // 16) // steps
 
     def opening(t, _):
         conv(0, t)
         for i in range(per_chunk):
             at = pl.ds(pl.multiple_of((t * per_chunk + i) * chunk, chunk), chunk)
-            for top in range(2):
-                mid_perm[top, :, at] = dot(mid[top * tall : (top + 1) * tall, at], swap[...]).astype(BF16)
+            mid_perm[:, at] = dot(mid[:, at], swap[...]).astype(BF16)
         return 0
 
     loads[4].wait()
     loads[5].wait()
-    lax.fori_loop(0, pieces, opening, 0)
+    lax.fori_loop(0, steps, opening, 0)
 
     loads[6].wait()
     repeat = (iota((features, latc), 0) >> shift_of(quads) == iota((features, latc), 1)).astype(BF16)
     lat_rep[...] = dot(repeat, lat[...]).astype(BF16)
     loads[7].wait()
 
-    step_bits = shift_of(pieces)
+    step_bits = shift_of(steps)
 
     def both(t, acc):
         acc = gather_latent(jnp.maximum(t - 1, 0), acc)
-        conv(1 + (t >> step_bits), t & (pieces - 1))
+        conv(1 + (t >> step_bits), t & (steps - 1))
         return deep(t, acc)
 
-    middle = (groups - 2) * pieces
+    middle = (groups - 2) * steps
     acc = lax.fori_loop(0, middle, both, jnp.zeros((features, cells), F32))
 
     def with_carry(t, acc):
         @pl.when(me > 0)
         def _():
-            carry(t).wait_recv()
+            for p in range(pieces // steps):
+                carry(t * (pieces // steps) + p).wait_recv()
 
         acc = gather_latent(middle + t - 1, acc)
         conv(groups - 1, t)
         return deep(middle + t, acc)
 
-    acc = lax.fori_loop(0, pieces, with_carry, acc)
+    acc = lax.fori_loop(0, steps, with_carry, acc)
 
     def closing(t, acc):
-        acc = gather_latent(middle + pieces + t - 1, acc)
-        return deep(middle + pieces + t, acc)
-
-    acc = lax.fori_loop(0, 2 * SPAN, closing, acc)
-    latent = gather_latent(jnp.int32(2 * nframes - 1), acc).astype(BF16)
+        acc = gather_latent(middle + steps + t - 1, acc)
+        return deep(middle + steps + t, acc)
+
+    acc = lax.fori_loop(0, SPAN, closing, acc)
+    latent = gather_latent(jnp.int32(nframes - 1), acc).astype(BF16)
 
     quad = iota((features, rows), 0) & (quads - 1)
     picked = jnp.zeros((features, rows), F32)
@@ -245,7 +249,7 @@
     outbuf[...] = payload.reshape(n, cap, width)
 
     def exchange(k):
-        to = lax.rem(me + k, n)
+        to = wrap(me + k, n)
         return pltpu.make_async_remote_copy(
             src_ref=outbuf.at[to],
             dst_ref=inbuf.at[me],
@@ -309,12 +313,12 @@
             vmem((nframes // SPAN, SPAN * c1, kspan), BF16),
             vmem((c1, 128), F32),
             vmem((16 * blocks, 16 * blocks), BF16),
-            vmem((2, c2 // 2, mid.shape[1]), BF16),
+            vmem(mid.shape, BF16),
             vmem((features, lat.shape[1]), BF16),
             vmem((4, cells, rows), BF16),
             vmem((n * cap, rows), BF16),
             vmem((nframes, c1 // 16, blocks, 16, cells), BF16),
-            vmem((2, c2 // 2, cells), BF16),
+            vmem((2, c2, cells), BF16),
             vmem((n, cap, width), F32),
             vmem((n, cap, width), F32),
             pltpu.SemaphoreType.DMA((8,)),

time: 31.7 us -> 28.1 us (0.89)
  Pallas kernels: 29.8 us -> 26.2 us
    pallas_call x1, Pallas kernels: 29.8 us -> 26.2 us  [per_device(): pl.pallas_call(functools.partial(kernel, n, side), out_shape=jax.ShapeDty...]
where the time goes in v4:
time: 28.1 us; the launch traced here: 27.8 us
  Pallas kernels  26.2 us (93%)
  matrix products  1.63 us (6%)
    pallas_call x1, Pallas kernels, per_device(): pl.pallas_call(functools.partial(kernel, n, side), out_shape=jax.ShapeDty...  26.2 us
    dot_general x1, matrix products, per_device(): return jnp.dot(placed, pe, preferred_element_type=F32).astype(BF16)  1.63 us

profile of v4, /device:TPU:0, one launch (start us, length us, event | category | flops | bytes accessed | tf_op | source)
XLA Modules:
  0.0 27.8 jit_solution(1794755821875165036)
XLA Ops:
  0.0 0.0 copy-start
  0.0 26.2 %shard_map.91 = bf16[64,64]{1,0:T(8,128)(2,1)} custom-call(s32[4]{0:T(128)} %clip_ref.1, s32[1,64]{1,0:T(1,128)} %bitcast.6, f32[1,128]{1,0:T(1,128)} %bitcast.7, bf16[8,48,4096]{2,1,0:T(8,128)(2,1)} %frames_hbm.1, bf16[48,128]{1,0:T(8,128)(2,1)} %bitcast.5, bf16[3,128,128]{2,1,0:T(8,128)(2,1)} %time_hbm.1, bf16[512,2048]{1,0:T(8,128)(2,1)} %mid_hbm.1, ...), custom_call_target="tpu_custom_call" | custom-call | flops 5502926848 | bytes 5251072 | tf_op jit(solution)/shard_map/pallas_call | solution.py:299
  26.2 0.0 copy-done
  26.2 1.6 %convolution_convert_fusion = bf16[64,2048]{1,0:T(8,128)(2,1)} fusion(bf16[64,64]{1,0:T(8,128)(2,1)} %shard_map.91, bf16[64,2048]{1,0:T(8,128)(2,1)S(1)} %copy-done), kind=kOutput, calls=%fused_computation | convolution fusion | flops 16908288 | bytes 532480 | tf_op jit(solution)/shard_map/dot_general | solution.py:339
Async XLA Ops:
  0.0 26.2 %copy-start = (bf16[64,2048]{1,0:T(8,128)(2,1)S(1)}, bf16[64,2048]{1,0:T(8,128)(2,1)}, u32[]{:S(2)}) copy-start(bf16[64,2048]{1,0:T(8,128)(2,1)} %param.17) | copy-start | bytes 786436

commit v5 on v4

--- a/solution.py
+++ b/solution.py
@@ -51,7 +51,8 @@
     quads = 4
     features = quads * latc
     pieces = carry_send.shape[0]
-    steps = 2
+    steps = 1
+    units = SPAN // steps
     per_step = blocks // steps
     groups = nframes // SPAN
 
@@ -191,6 +192,13 @@
             m_ref[unit & 1, q : q + 32, :] = (part + part * jnp.tanh(part)).astype(BF16)
         return acc
 
+    def deeps(t, acc):
+        for i in range(units):
+            unit = t * units + i
+            acc = gather_latent(jnp.maximum(unit - 1, 0), acc)
+            acc = deep(unit, acc)
+        return acc
+
     chunk = swap.shape[0]
     per_chunk = (c1 // 16) // steps
 
@@ -213,9 +221,8 @@
     step_bits = shift_of(steps)
 
     def both(t, acc):
-        acc = gather_latent(jnp.maximum(t - 1, 0), acc)
         conv(1 + (t >> step_bits), t & (steps - 1))
-        return deep(t, acc)
+        return deeps(t, acc)
 
     middle = (groups - 2) * steps
     acc = lax.fori_loop(0, middle, both, jnp.zeros((features, cells), F32))
@@ -226,17 +233,14 @@
             for p in range(pieces // steps):
                 carry(t * (pieces // steps) + p).wait_recv()
 
-        acc = gather_latent(middle + t - 1, acc)
         conv(groups - 1, t)
-        return deep(middle + t, acc)
+        return deeps(middle + t, acc)
 
     acc = lax.fori_loop(0, steps, with_carry, acc)
 
-    def closing(t, acc):
-        acc = gather_latent(middle + steps + t - 1, acc)
-        return deep(middle + steps + t, acc)
-
-    acc = lax.fori_loop(0, SPAN, closing, acc)
+    acc = deeps(jnp.int32(middle + steps), acc)
+    for extra in range(1, steps):
+        acc = deeps(jnp.int32(middle + steps + extra), acc)
     latent = gather_latent(jnp.int32(nframes - 1), acc).astype(BF16)
 
     quad = iota((features, rows), 0) & (quads - 1)

time: 28.1 us -> 28.5 us (1.014)
  Pallas kernels: 26.2 us -> 26.6 us
    pallas_call x1, Pallas kernels: 26.2 us -> 26.6 us  [per_device(): pl.pallas_call(functools.partial(kernel, n, side), out_shape=jax.ShapeDty...]
where the time goes in v5:
time: 28.5 us; the launch traced here: 28.2 us
  Pallas kernels  26.6 us (93%)
  matrix products  1.63 us (6%)
    pallas_call x1, Pallas kernels, per_device(): pl.pallas_call(functools.partial(kernel, n, side), out_shape=jax.ShapeDty...  26.6 us
    dot_general x1, matrix products, per_device(): return jnp.dot(placed, pe, preferred_element_type=F32).astype(BF16)  1.63 us

profile of v5, /device:TPU:0, one launch (start us, length us, event | category | flops | bytes accessed | tf_op | source)
XLA Modules:
  0.0 28.2 jit_solution(15174004209277228390)
XLA Ops:
  0.0 0.0 copy-start
  0.0 26.6 %shard_map.91 = bf16[64,64]{1,0:T(8,128)(2,1)} custom-call(s32[4]{0:T(128)} %clip_ref.1, s32[1,64]{1,0:T(1,128)} %bitcast.6, f32[1,128]{1,0:T(1,128)} %bitcast.7, bf16[8,48,4096]{2,1,0:T(8,128)(2,1)} %frames_hbm.1, bf16[48,128]{1,0:T(8,128)(2,1)} %bitcast.5, bf16[3,128,128]{2,1,0:T(8,128)(2,1)} %time_hbm.1, bf16[512,2048]{1,0:T(8,128)(2,1)} %mid_hbm.1, ...), custom_call_target="tpu_custom_call" | custom-call | flops 5502926848 | bytes 5251072 | tf_op jit(solution)/shard_map/pallas_call | solution.py:303
  26.6 0.0 copy-done
  26.6 1.6 %convolution_convert_fusion = bf16[64,2048]{1,0:T(8,128)(2,1)} fusion(bf16[64,64]{1,0:T(8,128)(2,1)} %shard_map.91, bf16[64,2048]{1,0:T(8,128)(2,1)S(1)} %copy-done), kind=kOutput, calls=%fused_computation | convolution fusion | flops 16908288 | bytes 532480 | tf_op jit(solution)/shard_map/dot_general | solution.py:343
Async XLA Ops:
  0.0 26.6 %copy-start = (bf16[64,2048]{1,0:T(8,128)(2,1)S(1)}, bf16[64,2048]{1,0:T(8,128)(2,1)}, u32[]{:S(2)}) copy-start(bf16[64,2048]{1,0:T(8,128)(2,1)} %param.17) | copy-start | bytes 786436

commit v6 on v4

--- a/solution.py
+++ b/solution.py
@@ -37,7 +37,7 @@
     toeplitz, masked, wide_gain, swap, mid_perm, lat_rep, pick, select, s_ref, m_ref, outbuf, inbuf,
     load_sem, carry_send, carry_recv, send_sem, recv_sem,
 ):
-    me = lax.axis_index("tok")
+    me, grp = lax.axis_index("tok"), lax.axis_index("grp")
     nframes, cin, pos = frames_hbm.shape
     c1 = stem_hbm.shape[1]
     cells = side * side
@@ -65,18 +65,18 @@
         pltpu.make_async_copy(lat_hbm, lat, load_sem.at[6]),
         pltpu.make_async_copy(frames_hbm.at[4:nframes], frames.at[6 : nframes + 2], load_sem.at[7]),
     ]
+    barrier = pltpu.get_barrier_semaphore()
+
+    def greet(k, _):
+        pl.semaphore_signal(
+            barrier, inc=1, device_id=(grp, wrap(me + k, n)), device_id_type=pl.DeviceIdType.MESH
+        )
+        return 0
+
+    lax.fori_loop(1, n, greet, 0)
+
     for load in loads:
         load.start()
-
-    barrier = pltpu.get_barrier_semaphore()
-
-    def greet(k, _):
-        pl.semaphore_signal(
-            barrier, inc=1, device_id={"tok": wrap(me + k, n)}, device_id_type=pl.DeviceIdType.MESH
-        )
-        return 0
-
-    lax.fori_loop(1, n, greet, 0)
 
     @pl.when(me == 0)
     def _():
@@ -104,7 +104,7 @@
             dst_ref=frames.at[0:2, :, at],
             send_sem=carry_send.at[p],
             recv_sem=carry_recv.at[p],
-            device_id={"tok": wrap(me + 1, n)},
+            device_id=(grp, wrap(me + 1, n)),
             device_id_type=pl.DeviceIdType.MESH,
         )
 
@@ -174,8 +174,8 @@
                     scale = lax.rsqrt(jnp.sum(hj * hj, axis=0, keepdims=True) * (1.0 / c1) + 1e-6)
                     for q in range(c1 // 16):
                         x = hj[q * 16 : (q + 1) * 16] * scale * wide_gain[q * 16 : (q + 1) * 16, :]
-                        u = x + x * jnp.tanh(x)
-                        s_ref[first + j, q, ab, :, lane : lane + 128] = u.astype(BF16)
+                        x = x.astype(BF16)
+                        s_ref[first + j, q, ab, :, lane : lane + 128] = x + x * jnp.tanh(x)
 
     def frame_of(unit):
         return (SPAN + unit) & (nframes - 1)
@@ -187,8 +187,8 @@
     def deep(unit, acc):
         g = dot(mid_perm[...], s_ref[frame_of(unit)].reshape(c1 * blocks, cells))
         for q in range(0, c2, 32):
-            part = g[q : q + 32]
-            m_ref[unit & 1, q : q + 32, :] = (part + part * jnp.tanh(part)).astype(BF16)
+            part = g[q : q + 32].astype(BF16)
+            m_ref[unit & 1, q : q + 32, :] = part + part * jnp.tanh(part)
         return acc
 
     chunk = swap.shape[0]
@@ -255,7 +255,7 @@
             dst_ref=inbuf.at[me],
             send_sem=send_sem.at[k],
             recv_sem=recv_sem.at[k],
-            device_id={"tok": to},
+            device_id=(grp, to),
             device_id_type=pl.DeviceIdType.MESH,
         )
 

time: 28.1 us -> 27.9 us (level)
  no operation moved by 1% of the time
where the time goes in v6:
time: 27.9 us; the launch traced here: 27.7 us
  Pallas kernels  26 us (93%)
  matrix products  1.63 us (6%)
    pallas_call x1, Pallas kernels, per_device(): pl.pallas_call(functools.partial(kernel, n, side), out_shape=jax.ShapeDty...  26 us
    dot_general x1, matrix products, per_device(): return jnp.dot(placed, pe, preferred_element_type=F32).astype(BF16)  1.63 us

profile of v6, /device:TPU:0, one launch (start us, length us, event | category | flops | bytes accessed | tf_op | source)
XLA Modules:
  0.0 27.7 jit_solution(13803461054682330482)
XLA Ops:
  0.0 0.0 copy-start
  0.0 26.0 %shard_map.91 = bf16[64,64]{1,0:T(8,128)(2,1)} custom-call(s32[4]{0:T(128)} %clip_ref.1, s32[1,64]{1,0:T(1,128)} %bitcast.6, f32[1,128]{1,0:T(1,128)} %bitcast.7, bf16[8,48,4096]{2,1,0:T(8,128)(2,1)} %frames_hbm.1, bf16[48,128]{1,0:T(8,128)(2,1)} %bitcast.5, bf16[3,128,128]{2,1,0:T(8,128)(2,1)} %time_hbm.1, bf16[512,2048]{1,0:T(8,128)(2,1)} %mid_hbm.1, ...), custom_call_target="tpu_custom_call" | custom-call | flops 5502926848 | bytes 5251072 | tf_op jit(solution)/shard_map/pallas_call | solution.py:299
  26.0 0.0 copy-done
  26.1 1.6 %convolution_convert_fusion = bf16[64,2048]{1,0:T(8,128)(2,1)} fusion(bf16[64,64]{1,0:T(8,128)(2,1)} %shard_map.91, bf16[64,2048]{1,0:T(8,128)(2,1)S(1)} %copy-done), kind=kOutput, calls=%fused_computation | convolution fusion | flops 16908288 | bytes 532480 | tf_op jit(solution)/shard_map/dot_general | solution.py:339
Async XLA Ops:
  0.0 26.0 %copy-start = (bf16[64,2048]{1,0:T(8,128)(2,1)S(1)}, bf16[64,2048]{1,0:T(8,128)(2,1)}, u32[]{:S(2)}) copy-start(bf16[64,2048]{1,0:T(8,128)(2,1)} %param.17) | copy-start | bytes 786436

commit v7 on v6

--- a/solution.py
+++ b/solution.py
@@ -34,7 +34,7 @@
     n, side, clip_ref, slot_hbm, gain_hbm, frames_hbm, stem_hbm, time_hbm, mid_hbm, lat_hbm,
     out_ref,
     slot, gain, frames, stem, time, mid, lat,
-    toeplitz, masked, wide_gain, swap, mid_perm, lat_rep, pick, select, s_ref, m_ref, outbuf, inbuf,
+    toeplitz, masked, wide_gain, swap, mid_perm, lat_rep, pick, select, s_ref, m_ref, partial, outbuf, inbuf,
     load_sem, carry_send, carry_recv, send_sem, recv_sem,
 ):
     me, grp = lax.axis_index("tok"), lax.axis_index("grp")
@@ -174,8 +174,7 @@
                     scale = lax.rsqrt(jnp.sum(hj * hj, axis=0, keepdims=True) * (1.0 / c1) + 1e-6)
                     for q in range(c1 // 16):
                         x = hj[q * 16 : (q + 1) * 16] * scale * wide_gain[q * 16 : (q + 1) * 16, :]
-                        x = x.astype(BF16)
-                        s_ref[first + j, q, ab, :, lane : lane + 128] = x + x * jnp.tanh(x)
+                        s_ref[first + j, t, q, i, :, lane : lane + 128] = (x + x * jnp.tanh(x)).astype(BF16)
 
     def frame_of(unit):
         return (SPAN + unit) & (nframes - 1)
@@ -184,12 +183,20 @@
         at = frame_of(unit) * c2
         return acc + dot(lat_rep[:, pl.ds(pl.multiple_of(at, c2), c2)], m_ref[unit & 1])
 
+    def silu_to_m(unit, g):
+        for q in range(0, c2, 32):
+            part = g[q : q + 32]
+            m_ref[unit & 1, q : q + 32, :] = (part + part * jnp.tanh(part)).astype(BF16)
+
     def deep(unit, acc):
-        g = dot(mid_perm[...], s_ref[frame_of(unit)].reshape(c1 * blocks, cells))
-        for q in range(0, c2, 32):
-            part = g[q : q + 32].astype(BF16)
-            m_ref[unit & 1, q : q + 32, :] = part + part * jnp.tanh(part)
+        acc = gather_latent(jnp.maximum(unit - 1, 0), acc)
+        silu_to_m(unit, dot(mid_perm[...], s_ref[frame_of(unit)].reshape(c1 * blocks, cells)))
         return acc
+
+    depth = c1 * per_step
+
+    def deep_part(frame, t):
+        return dot(mid_perm[:, t * depth : (t + 1) * depth], s_ref[frame, t].reshape(depth, cells))
 
     chunk = swap.shape[0]
     per_chunk = (c1 // 16) // steps
@@ -197,8 +204,12 @@
     def opening(t, _):
         conv(0, t)
         for i in range(per_chunk):
-            at = pl.ds(pl.multiple_of((t * per_chunk + i) * chunk, chunk), chunk)
-            mid_perm[:, at] = dot(mid[:, at], swap[...]).astype(BF16)
+            q = t * per_chunk + i
+            ordered = dot(mid[:, pl.ds(pl.multiple_of(q * chunk, chunk), chunk)], swap[...]).astype(BF16)
+            part = chunk // steps
+            for side_by in range(steps):
+                at = pl.ds(pl.multiple_of(side_by * depth + q * part, part), part)
+                mid_perm[:, at] = ordered[:, side_by * part : (side_by + 1) * part]
         return 0
 
     loads[4].wait()
@@ -213,30 +224,30 @@
     step_bits = shift_of(steps)
 
     def both(t, acc):
-        acc = gather_latent(jnp.maximum(t - 1, 0), acc)
         conv(1 + (t >> step_bits), t & (steps - 1))
         return deep(t, acc)
 
     middle = (groups - 2) * steps
     acc = lax.fori_loop(0, middle, both, jnp.zeros((features, cells), F32))
 
-    def with_carry(t, acc):
+    acc = lax.fori_loop(middle, middle + SPAN, deep, acc)
+
+    for t in range(steps):
+
         @pl.when(me > 0)
-        def _():
+        def _(t=t):
             for p in range(pieces // steps):
                 carry(t * (pieces // steps) + p).wait_recv()
 
-        acc = gather_latent(middle + t - 1, acc)
         conv(groups - 1, t)
-        return deep(middle + t, acc)
-
-    acc = lax.fori_loop(0, steps, with_carry, acc)
-
-    def closing(t, acc):
-        acc = gather_latent(middle + steps + t - 1, acc)
-        return deep(middle + steps + t, acc)
-
-    acc = lax.fori_loop(0, SPAN, closing, acc)
+        if t < steps - 1:
+            for j in range(SPAN):
+                part = deep_part(j, t)
+                partial[j] = part if t == 0 else partial[j] + part
+    for j in range(SPAN):
+        unit = nframes - SPAN + j
+        acc = gather_latent(jnp.int32(unit - 1), acc)
+        silu_to_m(unit, partial[j] + deep_part(j, steps - 1))
     latent = gather_latent(jnp.int32(nframes - 1), acc).astype(BF16)
 
     quad = iota((features, rows), 0) & (quads - 1)
@@ -317,8 +328,9 @@
             vmem((features, lat.shape[1]), BF16),
             vmem((4, cells, rows), BF16),
             vmem((n * cap, rows), BF16),
-            vmem((nframes, c1 // 16, blocks, 16, cells), BF16),
+            vmem((nframes, 2, c1 // 16, blocks // 2, 16, cells), BF16),
             vmem((2, c2, cells), BF16),
+            vmem((SPAN, c2, cells), F32),
             vmem((n, cap, width), F32),
             vmem((n, cap, width), F32),
             pltpu.SemaphoreType.DMA((8,)),

time: 27.9 us -> 27.9 us (level)
  no operation moved by 1% of the time
where the time goes in v7:
time: 27.9 us; the launch traced here: 27.6 us
  Pallas kernels  26 us (93%)
  matrix products  1.63 us (6%)
    pallas_call x1, Pallas kernels, per_device(): pl.pallas_call(functools.partial(kernel, n, side), out_shape=jax.ShapeDty...  26 us
    dot_general x1, matrix products, per_device(): return jnp.dot(placed, pe, preferred_element_type=F32).astype(BF16)  1.63 us

profile of v7, /device:TPU:0, one launch (start us, length us, event | category | flops | bytes accessed | tf_op | source)
XLA Modules:
  0.0 27.6 jit_solution(6010284232098659087)
XLA Ops:
  0.0 0.0 copy-start
  0.0 26.0 %shard_map.91 = bf16[64,64]{1,0:T(8,128)(2,1)} custom-call(s32[4]{0:T(128)} %clip_ref.1, s32[1,64]{1,0:T(1,128)} %bitcast.6, f32[1,128]{1,0:T(1,128)} %bitcast.7, bf16[8,48,4096]{2,1,0:T(8,128)(2,1)} %frames_hbm.1, bf16[48,128]{1,0:T(8,128)(2,1)} %bitcast.5, bf16[3,128,128]{2,1,0:T(8,128)(2,1)} %time_hbm.1, bf16[512,2048]{1,0:T(8,128)(2,1)} %mid_hbm.1, ...), custom_call_target="tpu_custom_call" | custom-call | flops 5502926848 | bytes 5251072 | tf_op jit(solution)/shard_map/pallas_call | solution.py:310
  26.0 0.0 copy-done
  26.0 1.6 %convolution_convert_fusion = bf16[64,2048]{1,0:T(8,128)(2,1)} fusion(bf16[64,64]{1,0:T(8,128)(2,1)} %shard_map.91, bf16[64,2048]{1,0:T(8,128)(2,1)S(1)} %copy-done), kind=kOutput, calls=%fused_computation | convolution fusion | flops 16908288 | bytes 532480 | tf_op jit(solution)/shard_map/dot_general | solution.py:351
Async XLA Ops:
  0.0 26.0 %copy-start = (bf16[64,2048]{1,0:T(8,128)(2,1)S(1)}, bf16[64,2048]{1,0:T(8,128)(2,1)}, u32[]{:S(2)}) copy-start(bf16[64,2048]{1,0:T(8,128)(2,1)} %param.17) | copy-start | bytes 786436
